TPU v7x, 512 devices: a whole 4x4x16 slice. The times are simulated.
512 devices in a mesh: rows: 8 (over y, core), tp: 64 (over z, x).
Axes of the slice: x: 4, y: 4, z: 16, core: 2. Of those that a mesh axis runs over, the one named last changes fastest.
Arguments:
- hidden: bfloat16 [2, 1024, 16384], P(None, ('rows', 'tp')), may hold values from -6 to 6
- adapter_ids: int32 [1024, 1], P('rows'), may hold values from 0 to 63; in each aligned block of 128 rows (0 to 127, 128 to 255, ...) at most 8 rows name the same one
- key_weight: bfloat16 [16384, 1024], P('tp'), may hold values from -0.046875 to 0.046875
- value_weight: bfloat16 [16384, 1024], P('tp'), may hold values from -0.046875 to 0.046875
- adapter_down: bfloat16 [16384, 4096], P('rows', 'tp'), may hold values from -0.046875 to 0.046875
- adapter_up: bfloat16 [64, 64, 1024], P('tp'), may hold values from -0.75 to 0.75
Outputs:
- key_out: bfloat16 [2, 1024, 1024], P(None, ('rows', 'tp'))
- value_out: bfloat16 [2, 1024, 1024], P(None, ('rows', 'tp'))
Inputs may be any that keep to these rules, and one draw needn't show every extreme that they name: `adapter_ids`: in each aligned block of 128 rows no adapter is named by more than 8 rows, a bound that some block reaches.
All inputs are finite; a program needn't handle non-finite values.
Results may differ from a plain program's by a relative error of at most 0.0085.
Values may be sent and summed in bfloat16 or wider, within the bound.
A program may use at most 64 MiB of HBM per device.

v0:
```python
import jax
import jax.numpy as jnp
from jax import lax
from jax.sharding import PartitionSpec as P


def shards(hidden, adapter_ids, key_weight, value_weight, adapter_down, adapter_up):
    step_total, row_number, model_width = hidden.shape
    group_size = lax.axis_size("tp")
    owner = lax.axis_index("tp")
    slice_width = model_width // group_size
    row_ids = adapter_ids[:, 0]
    owned = row_ids == owner
    down_local = lax.all_gather(adapter_down, "rows", axis=0, tiled=True)
    up_local = adapter_up[0]
    whole = lax.all_gather(hidden, "tp", axis=1, tiled=True)
    sliced = lax.dynamic_slice_in_dim(whole, owner * slice_width, slice_width, 2)
    shrink = jnp.einsum(
        "sgd,dr->sgr", whole, down_local, preferred_element_type=jnp.float32
    ).astype(jnp.bfloat16)
    lowrank_in = jnp.where(owned[None, :, None], shrink, jnp.zeros_like(shrink))
    key_part = jnp.einsum("scd,dk->csk", sliced, key_weight, preferred_element_type=jnp.float32)
    value_part = jnp.einsum("scd,dk->csk", sliced, value_weight, preferred_element_type=jnp.float32)
    value_part = value_part + jnp.einsum(
        "scr,rk->csk", lowrank_in, up_local, preferred_element_type=jnp.float32
    )
    summed = lax.psum_scatter(
        jnp.concatenate([key_part, value_part], axis=2), "tp", scatter_dimension=0, tiled=True
    )
    key_width = key_weight.shape[1]
    key_out = jnp.transpose(summed[:, :, :key_width], (1, 0, 2)).astype(jnp.bfloat16)
    value_out = jnp.transpose(summed[:, :, key_width:], (1, 0, 2)).astype(jnp.bfloat16)
    return (key_out, value_out)


def solution(mesh):
    placed = (
        P(None, ("rows", "tp"), None),
        P("rows", None),
        P("tp", None),
        P("tp", None),
        P("rows", "tp"),
        P("tp", None, None),
    )
    return jax.shard_map(
        shards,
        mesh=mesh,
        in_specs=placed,
        out_specs=(P(None, ("rows", "tp"), None), P(None, ("rows", "tp"), None)),
        check_vma=False,
    )
```

profile of v0, /device:TPU:8, one launch (start us, length us, event | category | flops | bytes accessed | tf_op | source)
XLA Modules:
  0.0 528.0 jit_solution(13716031929668960915)
XLA Ops:
  7.2 0.0 copy-start
  7.2 0.0 all-gather.3.cloned.1.call-start
  7.2 1.7 copy.8
  8.9 0.0 all-gather.3.cloned.1.call-update
  9.0 0.0 all-gather.5.cloned.1.call-start
  9.0 0.7 all-gather.5.cloned.1.call-update
  9.7 1.3 dynamic-slice
  11.7 0.7 compare_bitcast_fusion
  12.3 0.0 copy-start.1
  12.3 0.0 copy-start.2
  12.3 160.2 %all-gather.3.cloned.1.call-done = bf16[2,128,16384]{2,0,1:T(2,128)(2,1)} async-done(((bf16[2,2,16384]{2,0,1:T(2,128)(2,1)}), bf16[2,128,16384]{2,0,1:T(2,128)(2,1)}) %all-gather.3.cloned.1.call-update) | async-done | bytes 8388624 | tf_op jit(solution)/shard_map/all_gather | solution.py:16
  172.6 11.9 %copy.9 = bf16[2,128,16384]{2,1,0:T(8,128)(2,1)} copy(bf16[2,128,16384]{2,0,1:T(2,128)(2,1)} %all-gather.3.cloned.1.call-done) | data formatting | bytes 16777216 | tf_op jit(solution)/shard_map/all_gather | solution.py:16
  184.5 0.0 copy-done
  184.5 1.2 fusion.11
  185.7 0.0 copy-done.1
  185.7 2.2 convolution_bitcast_fusion
  188.0 13.6 %all-gather.5.cloned.1.call-done = bf16[16384,64]{0,1:T(8,128)(2,1)} async-done(((bf16[2048,64]{0,1:T(8,128)(2,1)}), bf16[16384,64]{0,1:T(8,128)(2,1)}) %all-gather.5.cloned.1.call-update) | async-done | bytes 2097168 | tf_op jit(solution)/shard_map/all_gather | solution.py:14
  201.5 0.0 copy-done.2
  201.5 14.7 %fusion.2 = f32[128,2,1024]{2,0,1:T(8,128)} fusion(f32[2,128,1024]{2,1,0:T(8,128)S(1)} %fusion.11, bf16[16384,64]{0,1:T(8,128)(2,1)} %all-gather.5.cloned.1.call-done, bf16[1,64,1024]{2,1,0:T(8,128)(2,1)S(1)} %copy-done.2, pred[128]{0:T(512)(128)(4,1)S(1)} %compare_bitcast_fusion, bf16[2,128,16384]{2,0,1:T(2,128)(2,1)} %all-gather.3.cloned.1.call-done), kind=kOutput, calls=%fused_computation.4 | convolution fusion | flops 570720256 | bytes 12714112 | tf_op jit(solution)/shard_map/scr,rk->csk/dot_general | solution.py:24
  216.2 1.7 pad_maximum_fusion
  217.9 301.8 %all-reduce.2 = bf16[128,2,2048]{2,0,1:T(8,128)(2,1)} all-reduce(f32[128,2,2048]{2,0,1:T(8,128)S(1)} %pad_maximum_fusion), channel_id=2, replica_groups=mesh['rows'=8,'tp'=64] {'tp'}, use_global_device_ids=true, to_apply=%region_0.1.clone | all-reduce | flops 524288 | bytes 3145728
  519.7 0.9 dynamic-slice_convert_fusion
  520.6 0.6 slice_bitcast_fusion
Async XLA Ops:
  7.2 177.4 %copy-start = (bf16[256,1024]{1,0:T(8,128)(2,1)S(1)}, bf16[256,1024]{1,0:T(8,128)(2,1)}, u32[]{:S(2)}) copy-start(bf16[256,1024]{1,0:T(8,128)(2,1)} %param.9) | copy-start | bytes 1572868
  7.2 165.4 %all-gather.3.cloned.1.call-start = ((), (), s32[]{:S(2)}) async-start(), calls=%async_computation | async-start | bytes 8519680 | tf_op jit(solution)/shard_map/all_gather | solution.py:16
  9.0 192.6 %all-gather.5.cloned.1.call-start = ((), (), s32[]{:S(2)}) async-start(), calls=%async_computation.1 | async-start | bytes 2359296 | tf_op jit(solution)/shard_map/all_gather | solution.py:14
  12.3 173.4 %copy-start.1 = (bf16[256,1024]{1,0:T(8,128)(2,1)S(1)}, bf16[256,1024]{1,0:T(8,128)(2,1)}, u32[]{:S(2)}) copy-start(bf16[256,1024]{1,0:T(8,128)(2,1)} %param.8) | copy-start | bytes 1572868
  12.3 189.2 %copy-start.2 = (bf16[1,64,1024]{2,1,0:T(8,128)(2,1)S(1)}, bf16[1,64,1024]{2,1,0:T(8,128)(2,1)}, u32[]{:S(2)}) copy-start(bf16[1,64,1024]{2,1,0:T(8,128)(2,1)} %param.11) | copy-start | bytes 393220
Sparse Core Ops, SparseCore 0:
  11.0 161.5 all-gather.2
  174.7 26.7 all-gather.4
where the time goes:
time: 528 us
  blocking collectives  302 us (57%)
  waiting for transfers between devices  175 us (33%)
  matrix products  18.1 us (3%)
  local copies, waits for them, and re-layouts  16.4 us (3%)
  between operations  14.7 us (3%)
    unnamed x1, blocking collectives  302 us
    all_gather x1, waiting for transfers between devices, shards(): whole = lax.all_gather(hidden, 'tp', axis=1, tiled=True)  160 us
    dot_general x1, matrix products, shards(): jnp.einsum('scr,rk->csk', lowrank_in, up_local, preferred_element_type=jn...  14.7 us
    all_gather x1, waiting for transfers between devices, shards(): down_local = lax.all_gather(adapter_down, 'rows', axis=0, tiled=True)  13.6 us
    all_gather x1, local copies, waits for them, and re-layouts, shards(): whole = lax.all_gather(hidden, 'tp', axis=1, tiled=True)  11.9 us
  transfers between devices with their start and end apart: 2, of which 2 were waited for; matrix products, arithmetic and copies ran while one was open for 3% of the time, Pallas kernels for 0%

commit v1 on v0

v1 whole, which is shorter than its diff:
```python
import functools

import jax
import jax.numpy as jnp
from jax import lax
from jax.experimental import pallas as pl
from jax.experimental.pallas import tpu as pltpu
from jax.sharding import PartitionSpec as P

MESH = pl.DeviceIdType.MESH
BF16 = jnp.bfloat16
F32 = jnp.float32
CORES = 2
SLOTS = 8
RANK = 64


def dot(a, b):
    return jnp.dot(a, b, preferred_element_type=F32)


def dot_t(a, b):
    return lax.dot_general(a, b, (((1,), (1,)), ((), ())), preferred_element_type=F32)


def log2(n):
    return n.bit_length() - 1


def kernel(
    nr, nz, nx,
    x_ref, idr_ref, idc_ref, wk_ref, wv_ref, dn_ref, up_ref,
    ko_ref, vo_ref,
    xg, wkg, wvg, ug, dsp, dg, xm, ss, sr, sh, ks, kr, vs, vr, og,
    loc, xz_s, xz_r, xx_s, xx_r, wk_s, wk_r, wv_s, wv_r, up_s, up_r,
    dr_s, dr_r, dz_s, dz_r, dy_s, dy_r, dc_s, dc_r,
    s_s, s_r, sh_s, sh_r, k_s, k_r, v_s, v_r, o_s, o_r,
):
    ny = nr // CORES
    lbs = x_ref.shape[1] // 4
    width = wkg.shape[2]
    fe = dn_ref.shape[3]
    rows = nz * nx * 4
    i = lax.axis_index("rows")
    p = lax.axis_index("tp")
    y, c = i // CORES, i % CORES
    z, x = p // nx, p % nx

    def at_z(k):
        return lax.rem(z + k, nz)

    def at_x(k):
        return lax.rem(x + k, nx)

    def z_dev(zz):
        return (i, zz * nx + x)

    def x_dev(xx):
        return (i, z * nx + xx)

    def r_dev(ii):
        return (ii, p)

    def send(src, dst, ss_, rs_, dev):
        return pltpu.make_async_remote_copy(
            src_ref=src, dst_ref=dst, send_sem=ss_, recv_sem=rs_, device_id=dev, device_id_type=MESH
        )

    barrier = pltpu.get_barrier_semaphore()
    for k in range(1, nr):
        pl.semaphore_signal(barrier, inc=1, device_id=r_dev(lax.rem(i + k, nr)), device_id_type=MESH)
    for k in range(1, nx):
        pl.semaphore_signal(barrier, inc=1, device_id=x_dev(at_x(k)), device_id_type=MESH)

    def greet(k, carry):
        pl.semaphore_signal(barrier, inc=1, device_id=z_dev(at_z(k)), device_id_type=MESH)
        return carry

    lax.fori_loop(1, nz, greet, 0)
    pl.semaphore_wait(barrier, nr + nx + nz - 3)

    def xz_copy(k, to):
        return send(x_ref.at[to], xg.at[x, z], xz_s.at[k], xz_r.at[k], z_dev(to))

    lax.fori_loop(1, nz, lambda k, t: (xz_copy(k, at_z(k)).start(), t)[1], 0)
    x_own = pltpu.make_async_copy(x_ref.at[z], xg.at[x, z], loc.at[0])
    x_own.start()

    def dr_copy(k):
        to = lax.rem(i + k, nr)
        return send(dn_ref.at[to], dsp.at[pl.ds(2 * i, 2)], dr_s.at[k], dr_r.at[k], r_dev(to))

    for k in range(1, nr):
        dr_copy(k).start()
    d_own = pltpu.make_async_copy(dn_ref.at[i], dsp.at[pl.ds(2 * i, 2)], loc.at[1])
    d_own.start()

    def col(xx):
        return pl.ds(pl.multiple_of(xx * width, width), width)

    def w_copies(k):
        to = at_x(k)
        return (
            send(wk_ref.at[:, col(to)], wkg.at[x], wk_s.at[k], wk_r.at[k], x_dev(to)),
            send(wv_ref.at[:, col(to)], wvg.at[x], wv_s.at[k], wv_r.at[k], x_dev(to)),
            send(up_ref.at[:, col(to)], ug.at[x], up_s.at[k], up_r.at[k], x_dev(to)),
        )

    for k in range(1, nx):
        for one in w_copies(k):
            one.start()
    w_own = (
        pltpu.make_async_copy(wk_ref.at[:, col(x)], wkg.at[x], loc.at[2]),
        pltpu.make_async_copy(wv_ref.at[:, col(x)], wvg.at[x], loc.at[3]),
        pltpu.make_async_copy(up_ref.at[:, col(x)], ug.at[x], loc.at[4]),
    )
    for one in w_own:
        one.start()

    for k in range(1, nr):
        dr_copy(k).wait_recv()
    d_own.wait()

    def dz_copy(k, to):
        return send(dsp.at[to], dg.at[i, z], dz_s.at[k], dz_r.at[k], z_dev(to))

    lax.fori_loop(1, nz, lambda k, t: (dz_copy(k, at_z(k)).start(), t)[1], 0)
    e_own = pltpu.make_async_copy(dsp.at[z], dg.at[i, z], loc.at[5])
    e_own.start()

    lax.fori_loop(1, nz, lambda k, t: (xz_copy(k, at_z(k)).wait_recv(), t)[1], 0)
    x_own.wait()

    def xx_copy(k):
        return send(xg.at[x], xg.at[x], xx_s.at[k], xx_r.at[k], x_dev(at_x(k)))

    for k in range(1, nx):
        xx_copy(k).start()

    bits_x, bits_lb = log2(nx), log2(lbs)
    idr, idc = idr_ref[...], idc_ref[...]
    rho_r = lax.broadcasted_iota(jnp.int32, (rows, rows), 1)
    rho_c = lax.broadcasted_iota(jnp.int32, (rows, rows), 0)
    same = (idr == idc) & (((rho_r ^ rho_c) & 2) == 0)
    slot_r = jnp.sum((same & (rho_c < rho_r)).astype(F32), axis=0, keepdims=True).astype(jnp.int32)
    slot_c = jnp.sum((same & (rho_r < rho_c)).astype(F32), axis=1, keepdims=True).astype(jnp.int32)
    slots = 2 * nz * SLOTS
    sig = lax.broadcasted_iota(jnp.int32, (slots, rows), 0)
    rho = lax.broadcasted_iota(jnp.int32, (slots, rows), 1)
    half = nz * SLOTS
    t_sig = (sig >= half).astype(jnp.int32)
    za_sig = (sig & (half - 1)) >> 3
    gather = (
        (idr == za_sig * nx + x) & (slot_r == (sig & (SLOTS - 1))) & (((rho >> 1) & 1) == t_sig)
    ).astype(F32).astype(BF16)

    block = 2 * nx * 4 * lbs
    o = lax.broadcasted_iota(jnp.int32, (block, block), 0)
    n = lax.broadcasted_iota(jnp.int32, (block, block), 1)
    r_o = o & 3
    x_o = (o >> 2) & (nx - 1)
    z_o = (o >> (2 + bits_x)) & 1
    l_o = o >> (3 + bits_x)
    perm = (n == ((((x_o * 2 + z_o) * 4 + r_o) << bits_lb) + l_o)).astype(F32).astype(BF16)

    def dy_copy(j, zz):
        to = lax.rem(y + j, ny) * CORES + c
        return send(dg.at[i, zz], dg.at[i, zz], dy_s.at[j], dy_r.at[j], r_dev(to))

    def forward(k, t):
        zz = lax.rem(z + nz - k, nz)
        dz_copy(k, zz).wait_recv()
        for j in range(1, ny):
            dy_copy(j, zz).start()
        return t

    e_own.wait()
    for j in range(1, ny):
        dy_copy(j, z).start()
    lax.fori_loop(1, nz // 2, forward, 0)

    for k in range(1, nx):
        xx_copy(k).wait_recv()
    zb = nz // 2
    wide = jnp.concatenate(
        [xg[:, 2 * b:2 * b + 2].reshape(block, 128) for b in range(zb)], axis=1
    )
    turned = dot(perm, wide).astype(BF16)
    part = 8 * nx
    for b in range(zb):
        for lb in range(lbs):
            xm[b * part:(b + 1) * part, lb * 128:(lb + 1) * 128] = turned[
                lb * part:(lb + 1) * part, b * 128:(b + 1) * 128
            ]
    for k in range(1, nx):
        for one in w_copies(k):
            one.wait_recv()
    for one in w_own:
        one.wait()
    per = rows // nz
    kp = dot(xm[...], wkg[...].reshape(nx * wkg.shape[1], width))
    ks[...] = kp.astype(BF16).reshape(nz, per, width)

    lax.fori_loop(nz // 2, nz, forward, 0)

    def k_copy(k, to):
        return send(ks.at[to], kr.at[z], k_s.at[k], k_r.at[k], z_dev(to))

    lax.fori_loop(1, nz, lambda k, t: (k_copy(k, at_z(k)).start(), t)[1], 0)
    kr[z] = ks[z]

    def dc_copy(j):
        e = lax.rem(y + ny - j, ny) * CORES + c
        return send(dg.at[e], dg.at[e], dc_s.at[j], dc_r.at[j], r_dev(y * CORES + 1 - c))

    def dy_whole(j):
        e = lax.rem(y + ny - j, ny) * CORES + c
        return send(dg.at[e], dg.at[e], dy_s.at[j], dy_r.at[j], r_dev(lax.rem(y + j, ny) * CORES + c))

    dc_copy(0).start()
    vp = dot(xm[...], wvg[...].reshape(nx * wvg.shape[1], width))
    picked = dot(gather, xm[...]).astype(BF16)
    for j in range(1, ny):
        dy_whole(j).wait_recv()
        dc_copy(j).start()
    for j in range(ny):
        dc_copy(j).wait_recv()

    cols = nz * RANK
    acc = jnp.zeros((slots, cols), F32)
    for e in range(nr):
        acc = acc + dot_t(picked[:, e * fe:(e + 1) * fe], dg[e].reshape(cols, fe))
    for a in range(nz):
        first = acc[a * SLOTS:(a + 1) * SLOTS, a * RANK:(a + 1) * RANK]
        second = acc[half + a * SLOTS:half + (a + 1) * SLOTS, a * RANK:(a + 1) * RANK]
        ss[a] = jnp.concatenate([first, second], axis=1)

    def s_copy(k, to):
        return send(ss.at[to], sr.at[z], s_s.at[k], s_r.at[k], z_dev(to))

    lax.fori_loop(1, nz, lambda k, t: (s_copy(k, at_z(k)).start(), t)[1], 0)
    sr[z] = ss[z]
    lax.fori_loop(1, nz, lambda k, t: (s_copy(k, at_z(k)).wait_recv(), t)[1], 0)
    sh[x] = jnp.sum(sr[...], axis=0).astype(BF16).astype(F32)

    def sh_copy(k):
        return send(sh.at[x], sh.at[x], sh_s.at[k], sh_r.at[k], x_dev(at_x(k)))

    for k in range(1, nx):
        sh_copy(k).start()
    spot = lax.broadcasted_iota(jnp.int32, (rows, nx * SLOTS), 1)
    place = (
        (idc == z * nx + (spot >> 3)) & (slot_c == (spot & (SLOTS - 1)))
    ).astype(F32).astype(BF16)
    lane = lax.broadcasted_iota(jnp.int32, (rows, 2 * RANK), 1)
    rho_l = lax.broadcasted_iota(jnp.int32, (rows, 2 * RANK), 0)
    mine = ((rho_l >> 1) & 1) == (lane >= RANK).astype(jnp.int32)
    for k in range(1, nx):
        sh_copy(k).wait_recv()
    low = jnp.where(mine, dot(place, sh[...].reshape(nx * SLOTS, 2 * RANK).astype(BF16)), 0.0)
    for xa in range(nx):
        low_a = jnp.where(idc == z * nx + xa, low, 0.0).astype(BF16)
        vp = vp + dot(low_a, jnp.concatenate([ug[xa], ug[xa]], axis=0))
    vs[...] = vp.astype(BF16).reshape(nz, per, width)

    def v_copy(k, to):
        return send(vs.at[to], vr.at[z], v_s.at[k], v_r.at[k], z_dev(to))

    lax.fori_loop(1, nz, lambda k, t: (v_copy(k, at_z(k)).start(), t)[1], 0)
    vr[z] = vs[z]
    lax.fori_loop(1, nz, lambda k, t: (k_copy(k, at_z(k)).wait_recv(), t)[1], 0)
    k_sum = jnp.sum(kr[...].astype(F32), axis=0)
    lax.fori_loop(1, nz, lambda k, t: (v_copy(k, at_z(k)).wait_recv(), t)[1], 0)
    v_sum = jnp.sum(vr[...].astype(F32), axis=0)
    og[x] = jnp.concatenate([k_sum, v_sum], axis=1).astype(BF16)

    def o_copy(k):
        return send(og.at[x], og.at[x], o_s.at[k], o_r.at[k], x_dev(at_x(k)))

    for k in range(1, nx):
        o_copy(k).start()

    def left(k, t):
        xz_copy(k, at_z(k)).wait_send()
        dz_copy(k, at_z(k)).wait_send()
        s_copy(k, at_z(k)).wait_send()
        k_copy(k, at_z(k)).wait_send()
        v_copy(k, at_z(k)).wait_send()
        return t

    lax.fori_loop(1, nz, left, 0)
    for k in range(1, nr):
        dr_copy(k).wait_send()
    for k in range(1, nx):
        for one in w_copies(k):
            one.wait_send()
        xx_copy(k).wait_send()
        sh_copy(k).wait_send()
    for j in range(1, ny):
        dy_whole(j).wait_send()
    for j in range(ny):
        dc_copy(j).wait_send()

    for k in range(1, nx):
        o_copy(k).wait_recv()
    want = lax.broadcasted_iota(jnp.int32, (8, per), 1) == (
        lax.broadcasted_iota(jnp.int32, (8, per), 0) + 4 * x
    )
    want = want.astype(F32).astype(BF16)
    for xx in range(nx):
        mine4 = dot(want, og[xx])[:4].astype(BF16)
        ko_ref[:, xx * width:(xx + 1) * width] = mine4[:, :width]
        vo_ref[:, xx * width:(xx + 1) * width] = mine4[:, width:]
    for k in range(1, nx):
        o_copy(k).wait_send()


def shards(nr, nz, nx, hidden, adapter_ids, key_weight, value_weight, adapter_down, adapter_up):
    steps, own, wide = hidden.shape
    width = key_weight.shape[1] // nx
    deep = key_weight.shape[0]
    fz = wide // nz
    lbs = fz // 128
    fe = fz // nr
    rows = nz * nx * 4
    xz = hidden.reshape(4, nz, lbs, 128).transpose(1, 0, 2, 3).reshape(nz, 4 * lbs, 128)
    ids = jnp.broadcast_to(adapter_ids.reshape(nz * nx, 1, own), (nz * nx, steps, own))
    dn = adapter_down.reshape(2, nr, fe, RANK).transpose(1, 0, 3, 2)
    any_, vmem = pl.BlockSpec(memory_space=pl.ANY), pl.BlockSpec(memory_space=pltpu.VMEM)
    dma = pltpu.SemaphoreType.DMA
    per = rows // nz
    key_out, value_out = pl.pallas_call(
        functools.partial(kernel, nr, nz, nx),
        out_shape=[jax.ShapeDtypeStruct((4, nx * width), BF16)] * 2,
        in_specs=[any_, vmem, vmem, any_, any_, any_, any_],
        out_specs=[vmem, vmem],
        scratch_shapes=[
            pltpu.VMEM((nx, nz, 4 * lbs, 128), BF16),
            pltpu.VMEM((nx, deep, width), BF16),
            pltpu.VMEM((nx, deep, width), BF16),
            pltpu.VMEM((nx, RANK, width), BF16),
            pltpu.VMEM((nz, RANK, fe), BF16),
            pltpu.VMEM((nr, nz, RANK, fe), BF16),
            pltpu.VMEM((rows, fz), BF16),
            pltpu.VMEM((nz, SLOTS, 2 * RANK), F32),
            pltpu.VMEM((nz, SLOTS, 2 * RANK), F32),
            pltpu.VMEM((nx, SLOTS, 2 * RANK), F32),
            pltpu.VMEM((nz, per, width), BF16),
            pltpu.VMEM((nz, per, width), BF16),
            pltpu.VMEM((nz, per, width), BF16),
            pltpu.VMEM((nz, per, width), BF16),
            pltpu.VMEM((nx, per, 2 * width), BF16),
            dma((6,)),
            dma((nz,)), dma((nz,)), dma((nx,)), dma((nx,)),
            dma((nx,)), dma((nx,)), dma((nx,)), dma((nx,)), dma((nx,)), dma((nx,)),
            dma((nr,)), dma((nr,)), dma((nz,)), dma((nz,)),
            dma((nr,)), dma((nr,)), dma((nr,)), dma((nr,)),
            dma((nz,)), dma((nz,)), dma((nx,)), dma((nx,)),
            dma((nz,)), dma((nz,)), dma((nz,)), dma((nz,)), dma((nx,)), dma((nx,)),
        ],
        compiler_params=pltpu.CompilerParams(
            collective_id=0, has_side_effects=True, vmem_limit_bytes=32 * 1024 * 1024
        ),
        cost_estimate=pl.CostEstimate(flops=2_000_000_000, bytes_accessed=4_000_000, transcendentals=0),
    )(xz, ids.reshape(1, rows), ids.reshape(rows, 1), key_weight, value_weight, dn, adapter_up[0])
    return key_out.reshape(steps, own, -1), value_out.reshape(steps, own, -1)


def solution(mesh):
    nr, tp = mesh.shape["rows"], mesh.shape["tp"]
    nx = 4 if tp >= 64 else 2
    placed = (
        P(None, ("rows", "tp"), None),
        P("rows", None),
        P("tp", None),
        P("tp", None),
        P("rows", "tp"),
        P("tp", None, None),
    )
    return jax.shard_map(
        functools.partial(shards, nr, tp // nx, nx),
        mesh=mesh,
        in_specs=placed,
        out_specs=(P(None, ("rows", "tp"), None), P(None, ("rows", "tp"), None)),
        check_vma=False,
    )
```

time: 528 us -> 83 us (0.16)
  the two profiles are of different devices: /device:TPU:8 before, /device:TPU:1 now
where the time goes in v1:
time: 83 us; the launch traced here: 82.9 us
  Pallas kernels  77.9 us (94%)
  local copies, waits for them, and re-layouts  3.58 us (4%)
    pallas_call x1, Pallas kernels, shards(): pl.pallas_call(functools.partial(kernel, nr, nz, nx), out_shape=[jax.Shap...  77.9 us
    unnamed x14, local copies, waits for them, and re-layouts  1.73 us

profile of v1, /device:TPU:1, one launch (start us, length us, event | category | flops | bytes accessed | tf_op | source)
XLA Modules:
  0.0 82.9 jit_solution(12781842993368418883)
XLA Ops:
  0.6 0.0 copy-start.5
  0.6 0.0 copy-start.3
  0.6 0.5 broadcast.3
  1.2 0.1 copy-done.5
  1.3 0.7 reduce.3
  1.9 0.1 broadcast_in_dim.7
  2.1 0.1 reshape.34.idc_ref
  2.3 0.1 reshape.29.idr_ref
  2.4 0.0 copy-done.3
  2.4 0.0 copy-start.4
  2.4 0.0 copy-start.2
  2.5 0.0 copy-start
  2.5 0.0 copy-start.1
  2.5 0.1 copy.15
  2.6 0.7 copy-done.4
  3.3 0.1 reshape.27
  3.5 0.0 copy-done.2
  3.5 0.1 copy-done
  3.6 0.2 copy-done.1
  3.8 77.9 %shard_map.77 = (bf16[4,1024]{1,0:T(4,128)(2,1)S(1)}, bf16[4,1024]{1,0:T(4,128)(2,1)S(1)}) custom-call(bf16[16,32,128]{2,1,0:T(8,128)(2,1)S(1)} %bitcast.16, s32[1,256]{1,0:T(1,128)S(1)} %reshape.29.idr_ref, s32[256,1]{1,0:T(8,128)S(1)} %reshape.34.idc_ref, bf16[256,1024]{1,0:T(8,128)(2,1)S(1)} %copy-done, bf16[256,1024]{1,0:T(8,128)(2,1)S(1)} %copy-done.1, ...), custom_call_target="tpu_custom_call" | custom-call | flops 2000000000 | bytes 4000000 | tf_op jit(solution)/shard_map/pallas_call | solution.py:332
  81.7 0.6 reshape.32
  82.3 0.6 reshape.33
  (3 shorter events, 0.1 us)
Async XLA Ops:
  0.6 0.7 copy-start.5
  0.6 1.8 %copy-start.3 = (bf16[2048,64]{0,1:T(8,128)(2,1)S(1)}, bf16[2048,64]{0,1:T(8,128)(2,1)}, u32[]{:S(2)}) copy-start(bf16[2048,64]{0,1:T(8,128)(2,1)} %param.10) | copy-start | bytes 786436
  2.4 0.9 %copy-start.4 = (bf16[2,2,16384]{2,1,0:T(2,128)(2,1)S(1)}, bf16[2,2,16384]{2,1,0:T(2,128)(2,1)}, u32[]{:S(2)}) copy-start(bf16[2,2,16384]{2,1,0:T(2,128)(2,1)} %param.6) | copy-start | bytes 393220
  2.4 1.0 %copy-start.2 = (bf16[1,64,1024]{2,1,0:T(8,128)(2,1)S(1)}, bf16[1,64,1024]{2,1,0:T(8,128)(2,1)}, u32[]{:S(2)}) copy-start(bf16[1,64,1024]{2,1,0:T(8,128)(2,1)} %param.11) | copy-start | bytes 393220
  2.5 1.1 %copy-start = (bf16[256,1024]{1,0:T(8,128)(2,1)S(1)}, bf16[256,1024]{1,0:T(8,128)(2,1)}, u32[]{:S(2)}) copy-start(bf16[256,1024]{1,0:T(8,128)(2,1)} %wk_ref.1) | copy-start | bytes 1572868
  2.5 1.3 %copy-start.1 = (bf16[256,1024]{1,0:T(8,128)(2,1)S(1)}, bf16[256,1024]{1,0:T(8,128)(2,1)}, u32[]{:S(2)}) copy-start(bf16[256,1024]{1,0:T(8,128)(2,1)} %wv_ref.1) | copy-start | bytes 1572868

commit v2 on v0

v2 whole, which is shorter than its diff:
```python
import functools

import jax
import jax.numpy as jnp
from jax import lax
from jax.experimental import pallas as pl
from jax.experimental.pallas import tpu as pltpu
from jax.sharding import PartitionSpec as P

MESH = pl.DeviceIdType.MESH
BF16 = jnp.bfloat16
F32 = jnp.float32
CORES = 2
SLOTS = 8
RANK = 64


def dot(a, b):
    return jnp.dot(a, b, preferred_element_type=F32)


def dot_t(a, b):
    return lax.dot_general(a, b, (((1,), (1,)), ((), ())), preferred_element_type=F32)


def log2(n):
    return n.bit_length() - 1


TURNS = {16: (8, 7, 1, 0, 9, 6, 2, 15, 10, 5, 3, 14, 11, 4, 12, 13), 4: (2, 0, 1, 3)}


def kernel(
    nr, nz, nx, ng,
    x_ref, id_ref, wk_ref, wv_ref, dn_ref, up_ref,
    ko_ref, vo_ref,
    xg, wkg, wvg, ug, dsp, dg, xm, ss, sr, sh, ks, kr, vs, vr,
    loc, xz_s, xz_r, xx_s, xx_r, wk_s, wk_r, wv_s, wv_r, wkc_s, wkc_r, wvc_s, wvc_r, up_s, up_r, upc_s, upc_r,
    dr_s, dr_r, dz_s, dz_r, dy_s, dy_r, dc_s, dc_r,
    s_s, s_r, sh_s, sh_r, k_s, k_r, v_s, v_r,
):
    ny = nr // CORES
    qg = nz // ng
    lbs = x_ref.shape[1] // 4
    width = wkg.shape[2]
    lbo = width // 128
    fe = dn_ref.shape[3]
    rows = nz * nx * 4
    i = lax.axis_index("rows")
    p = lax.axis_index("tp")
    y, c = i // CORES, i % CORES
    z, x = p // nx, p % nx
    far = nz // 2

    def step(q):
        return far + (1 - 2 * (q % 2)) * ((q + 1) // 2)

    def to_z(q):
        return (z + step(q)) % nz

    hops = TURNS[nz]

    def at_x(k):
        return (x + k) % nx

    def z_dev(zz):
        return (i, zz * nx + x)

    def x_dev(xx):
        return (i, z * nx + xx)

    def r_dev(ii):
        return (ii, p)

    other = r_dev(y * CORES + 1 - c)

    def send(src, dst, ss_, rs_, dev):
        return pltpu.make_async_remote_copy(
            src_ref=src, dst_ref=dst, send_sem=ss_, recv_sem=rs_, device_id=dev, device_id_type=MESH
        )

    def turns(body):
        def one(q, t):
            body(q)
            return t

        lax.fori_loop(0, nz - 1, one, 0)

    barrier = pltpu.get_barrier_semaphore()
    turns(lambda q: pl.semaphore_signal(barrier, inc=1, device_id=z_dev(to_z(q)), device_id_type=MESH))
    for k in range(1, nr):
        pl.semaphore_signal(barrier, inc=1, device_id=r_dev((i + k) % nr), device_id_type=MESH)
    for k in range(1, nx):
        pl.semaphore_signal(barrier, inc=1, device_id=x_dev(at_x(k)), device_id_type=MESH)

    x_own = pltpu.make_async_copy(x_ref.at[z], xg.at[x, z], loc.at[0])
    d_own = pltpu.make_async_copy(dn_ref.at[i], dsp.at[pl.ds(2 * i, 2)], loc.at[1])
    w_own = (
        pltpu.make_async_copy(wk_ref, wkg.at[x], loc.at[2]),
        pltpu.make_async_copy(wv_ref, wvg.at[x], loc.at[3]),
        pltpu.make_async_copy(up_ref, ug.at[x], loc.at[4]),
    )
    for one in (x_own, d_own) + w_own:
        one.start()

    pl.semaphore_wait(barrier, nr + nx + nz - 3)

    def xz_copy(q):
        return send(x_ref.at[to_z(q)], xg.at[x, z], xz_s.at[q], xz_r.at[q], z_dev(to_z(q)))

    def dr_copy(k):
        to = (i + k) % nr
        return send(dn_ref.at[to], dsp.at[pl.ds(2 * i, 2)], dr_s.at[k], dr_r.at[k], r_dev(to))

    for k in range(1, nr):
        dr_copy(k).start()
    turns(lambda q: xz_copy(q).start())

    deep = wk_ref.shape[0]

    def share(n):
        return pl.ds(pl.multiple_of(c * (n // CORES), n // CORES), n // CORES)

    def wk_copy(k):
        some = share(deep)
        return send(wk_ref.at[some], wkg.at[x, some], wk_s.at[k], wk_r.at[k], x_dev(at_x(k)))

    def wv_copy(k):
        some = share(deep)
        return send(wv_ref.at[some], wvg.at[x, some], wv_s.at[k], wv_r.at[k], x_dev(at_x(k)))

    def up_copy(k):
        some = share(RANK)
        return send(up_ref.at[some], ug.at[x, some], up_s.at[k], up_r.at[k], x_dev(at_x(k)))

    def pass_on(ref, n, s_sem, r_sem, k):
        xx, some = (x + nx - k) % nx, share(n)
        return send(ref.at[xx, some], ref.at[xx, some], s_sem.at[k], r_sem.at[k], other)

    def wkc_copy(k):
        return pass_on(wkg, deep, wkc_s, wkc_r, k)

    def wvc_copy(k):
        return pass_on(wvg, deep, wvc_s, wvc_r, k)

    def upc_copy(k):
        return pass_on(ug, RANK, upc_s, upc_r, k)

    for k in range(1, nx):
        wk_copy(k).start()

    group = rows // 2
    ids = jnp.broadcast_to(id_ref[...].astype(F32).astype(BF16), (8, group))
    r_a = lax.broadcasted_iota(jnp.int32, (group, rows), 0)
    n_a = lax.broadcasted_iota(jnp.int32, (group, rows), 1)
    idr = dot(ids, (r_a == (n_a >> 2) * 2 + (n_a & 1)).astype(F32).astype(BF16))[:1].astype(jnp.int32)
    r_b = lax.broadcasted_iota(jnp.int32, (rows, group), 1)
    n_b = lax.broadcasted_iota(jnp.int32, (rows, group), 0)
    idc = dot_t((r_b == (n_b >> 2) * 2 + (n_b & 1)).astype(F32).astype(BF16), ids)[:, :1].astype(jnp.int32)

    bits_x, bits_lb = log2(nx), log2(lbs)
    rho_r = lax.broadcasted_iota(jnp.int32, (rows, rows), 1)
    rho_c = lax.broadcasted_iota(jnp.int32, (rows, rows), 0)
    same = (idr == idc) & (((rho_r ^ rho_c) & 2) == 0)
    slot_r = jnp.sum((same & (rho_c < rho_r)).astype(F32), axis=0, keepdims=True).astype(jnp.int32)
    slot_c = jnp.sum((same & (rho_r < rho_c)).astype(F32), axis=1, keepdims=True).astype(jnp.int32)
    half = qg * SLOTS
    slots = 2 * nz * SLOTS
    sig = lax.broadcasted_iota(jnp.int32, (slots, rows), 0)
    rho = lax.broadcasted_iota(jnp.int32, (slots, rows), 1)
    t_sig = (sig >> log2(half)) & 1
    col_sig = lax.broadcasted_iota(jnp.int32, (slots, 1), 0)
    q_sig = (col_sig >> log2(2 * half)) * qg + ((col_sig & (half - 1)) >> 3)
    za_sig = jnp.zeros((slots, 1), jnp.int32)
    for q in range(nz):
        za_sig = jnp.where(q_sig == q, (z + nz - hops[q]) % nz, za_sig)
    gather = (
        (idr == za_sig * nx + x) & (slot_r == (sig & (SLOTS - 1))) & (((rho >> 1) & 1) == t_sig)
    ).astype(F32).astype(BF16)
    spot = lax.broadcasted_iota(jnp.int32, (rows, nx * SLOTS), 1)
    place = (
        (idc == z * nx + (spot >> 3)) & (slot_c == (spot & (SLOTS - 1)))
    ).astype(F32).astype(BF16)

    block = 2 * nx * 4 * lbs
    o = lax.broadcasted_iota(jnp.int32, (block, block), 0)
    n = lax.broadcasted_iota(jnp.int32, (block, block), 1)
    r_o = o & 3
    x_o = (o >> 2) & (nx - 1)
    z_o = (o >> (2 + bits_x)) & 1
    l_o = o >> (3 + bits_x)
    perm = (n == ((((x_o * 2 + z_o) * 4 + r_o) << bits_lb) + l_o)).astype(F32).astype(BF16)

    tail = nz * 4
    o_own = lax.broadcasted_iota(jnp.int32, (tail, rows), 0)
    n_own = lax.broadcasted_iota(jnp.int32, (tail, rows), 1)
    own = (n_own == (o_own >> 2) * (4 * nx) + 4 * x + (o_own & 3)).astype(F32).astype(BF16)
    place = dot(own, place)
    big = tail * lbo
    o_out = lax.broadcasted_iota(jnp.int32, (big, big), 0)
    n_out = lax.broadcasted_iota(jnp.int32, (big, big), 1)
    spread = (
        n_out == (o_out & (lbo - 1)) * tail + (o_out >> log2(lbo))
    ).astype(F32).astype(BF16)

    def parcels(part):
        tall = jnp.concatenate([part[:, lb * 128:(lb + 1) * 128] for lb in range(lbo)], axis=0)
        return dot(spread, tall).astype(BF16).reshape(nz, 4 * lbo, 128)

    for k in range(1, nr):
        dr_copy(k).wait_recv()
    d_own.wait()

    def dz_copy(q):
        to = (z + hops[q]) % nz
        return send(dsp.at[to], dg.at[i, q], dz_s.at[q], dz_r.at[q], z_dev(to))

    def over_z(g):
        if g > 1:
            for q in range((g - 2) * qg, (g - 1) * qg):
                if hops[q]:
                    dz_copy(q).wait_send()
        for q in range(g * qg, (g + 1) * qg):
            if hops[q]:
                dz_copy(q).start()

    over_z(0)
    over_z(1)
    e_own = pltpu.make_async_copy(dsp.at[z], dg.at[i, hops.index(0)], loc.at[5])
    e_own.start()

    turns(lambda q: xz_copy(q).wait_recv())
    x_own.wait()

    def xx_copy(k):
        return send(xg.at[x], xg.at[x], xx_s.at[k], xx_r.at[k], x_dev(at_x(k)))

    for k in range(1, nx):
        xx_copy(k).start()

    def dy_copy(j, g):
        some = pl.ds(g * qg, qg)
        to = ((y + j) % ny) * CORES + c
        return send(dg.at[i, some], dg.at[i, some], dy_s.at[j, g], dy_r.at[j, g], r_dev(to))

    def dc_copy(j, g):
        some = pl.ds(g * qg, qg)
        e = ((y + ny - j) % ny) * CORES + c
        return send(dg.at[e, some], dg.at[e, some], dc_s.at[j, g], dc_r.at[j, g], other)

    def over_y(g):
        for q in range(g * qg, (g + 1) * qg):
            if hops[q]:
                dz_copy(q).wait_recv()
            else:
                e_own.wait()
        for j in range(1, ny):
            dy_copy(j, g).start()
        dc_copy(0, g).start()

    def over_core(g):
        for j in range(1, ny):
            dy_copy(j, g).wait_recv()
            dc_copy(j, g).start()

    def s_copy(q):
        return send(ss.at[q], sr.at[q], s_s.at[q], s_r.at[q], z_dev((z + nz - hops[q]) % nz))

    def shrink(g, picked):
        for j in range(ny):
            dc_copy(j, g).wait_recv()
        acc = jnp.zeros((2 * half, qg * RANK), F32)
        for e in range(nr):
            block_d = dg[e, g * qg:(g + 1) * qg].reshape(qg * RANK, fe)
            acc = acc + dot_t(picked[2 * half * g:2 * half * (g + 1), e * fe:(e + 1) * fe], block_d)
        for a in range(qg):
            first = acc[a * SLOTS:(a + 1) * SLOTS, a * RANK:(a + 1) * RANK]
            second = acc[half + a * SLOTS:half + (a + 1) * SLOTS, a * RANK:(a + 1) * RANK]
            q = g * qg + a
            if hops[q]:
                ss[q] = jnp.concatenate([first, second], axis=1)
                s_copy(q).start()
            else:
                sr[q] = jnp.concatenate([first, second], axis=1)

    def k_copy(q):
        return send(ks.at[to_z(q)], kr.at[q], k_s.at[q], k_r.at[q], z_dev(to_z(q)))

    for g in range(2, ng):
        over_z(g)
        over_y(g - 2)

    for k in range(1, nx):
        xx_copy(k).wait_recv()
    for k in range(1, nx):
        wv_copy(k).start()
        up_copy(k).start()
    for k in range(1, nx):
        wk_copy(k).wait_recv()
        wkc_copy(k).start()
    zb = nz // 2
    wide = jnp.concatenate(
        [xg[:, 2 * b:2 * b + 2].reshape(block, 128) for b in range(zb)], axis=1
    )
    turned = dot(perm, wide).astype(BF16)
    tall = 8 * nx
    for b in range(zb):
        for lb in range(lbs):
            xm[b * tall:(b + 1) * tall, lb * 128:(lb + 1) * 128] = turned[
                lb * tall:(lb + 1) * tall, b * 128:(b + 1) * 128
            ]
    picked = dot(gather, xm[...]).astype(BF16)

    for g in range(ng - 2):
        over_core(g)
    over_y(ng - 2)

    for k in range(1, nx):
        wkc_copy(k).wait_recv()
    for one in w_own:
        one.wait()
    x_rows = dot(own, xm[...]).astype(BF16)
    ks[...] = parcels(dot(x_rows, wkg[...].reshape(nx * deep, width)).astype(BF16))
    kr[nz - 1] = ks[z]
    over_y(ng - 1)
    over_core(ng - 2)
    turns(lambda q: k_copy(q).start())
    for g in range(ng - 2):
        shrink(g, picked)
    over_core(ng - 1)
    shrink(ng - 2, picked)
    shrink(ng - 1, picked)
    for k in range(1, nx):
        wv_copy(k).wait_recv()
        up_copy(k).wait_recv()
        wvc_copy(k).start()
        upc_copy(k).start()

    for q in range(nz):
        if hops[q]:
            s_copy(q).wait_recv()
    sh[x] = jnp.sum(sr[...], axis=0).astype(BF16).astype(F32)

    def sh_copy(k):
        return send(sh.at[x], sh.at[x], sh_s.at[k], sh_r.at[k], x_dev(at_x(k)))

    for k in range(1, nx):
        sh_copy(k).start()
    for k in range(1, nx):
        wvc_copy(k).wait_recv()
        upc_copy(k).wait_recv()
    vp = dot(x_rows, wvg[...].reshape(nx * deep, width))
    lane = lax.broadcasted_iota(jnp.int32, (tail, 2 * RANK), 1)
    row_l = lax.broadcasted_iota(jnp.int32, (tail, 2 * RANK), 0)
    mine = ((row_l >> 1) & 1) == (lane >= RANK).astype(jnp.int32)
    spot_o = lax.broadcasted_iota(jnp.int32, (tail, nx * SLOTS), 1) >> 3
    for k in range(1, nx):
        sh_copy(k).wait_recv()
    shrinks = sh[...].reshape(nx * SLOTS, 2 * RANK).astype(BF16)
    for xa in range(nx):
        place_a = jnp.where(spot_o == xa, place, 0.0).astype(BF16)
        low_a = jnp.where(mine, dot(place_a, shrinks), 0.0).astype(BF16)
        vp = vp + dot(low_a, jnp.concatenate([ug[xa], ug[xa]], axis=0))
    vs[...] = parcels(vp.astype(BF16))

    def v_copy(q):
        return send(vs.at[to_z(q)], vr.at[q], v_s.at[q], v_r.at[q], z_dev(to_z(q)))

    turns(lambda q: v_copy(q).start())
    vr[nz - 1] = vs[z]
    turns(lambda q: k_copy(q).wait_recv())
    ko_ref[...] = jnp.sum(kr[...].astype(F32), axis=0).astype(BF16)

    for k in range(1, nr):
        dr_copy(k).wait_send()
    for k in range(1, nx):
        for one in (wk_copy, wv_copy, up_copy, wkc_copy, wvc_copy, upc_copy):
            one(k).wait_send()
        xx_copy(k).wait_send()
        sh_copy(k).wait_send()
    for g in range(ng):
        for j in range(1, ny):
            dy_copy(j, g).wait_send()
        for j in range(ny):
            dc_copy(j, g).wait_send()

    def left(q):
        xz_copy(q).wait_send()
        k_copy(q).wait_send()

    turns(left)
    for q in range(nz):
        if hops[q]:
            s_copy(q).wait_send()
            if q >= (ng - 2) * qg:
                dz_copy(q).wait_send()

    turns(lambda q: v_copy(q).wait_recv())
    vo_ref[...] = jnp.sum(vr[...].astype(F32), axis=0).astype(BF16)
    turns(lambda q: v_copy(q).wait_send())


def shards(nr, nz, nx, hidden, adapter_ids, key_weight, value_weight, adapter_down, adapter_up):
    steps, own, wide = hidden.shape
    width = key_weight.shape[1]
    lbo = width // 128
    deep = key_weight.shape[0]
    fz = wide // nz
    lbs = fz // 128
    fe = fz // nr
    rows = nz * nx * 4
    xz = hidden.reshape(4, nz, lbs, 128).transpose(1, 0, 2, 3).reshape(nz, 4 * lbs, 128)
    dn = adapter_down.reshape(2, nr, fe, RANK).transpose(1, 0, 3, 2)
    any_, vmem = pl.BlockSpec(memory_space=pl.ANY), pl.BlockSpec(memory_space=pltpu.VMEM)
    dma = pltpu.SemaphoreType.DMA
    ng = 4 if nz >= 16 else 2
    ny = nr // CORES
    key_out, value_out = pl.pallas_call(
        functools.partial(kernel, nr, nz, nx, ng),
        out_shape=[jax.ShapeDtypeStruct((4 * lbo, 128), BF16)] * 2,
        in_specs=[any_, vmem, any_, any_, any_, any_],
        out_specs=[vmem, vmem],
        scratch_shapes=[
            pltpu.VMEM((nx, nz, 4 * lbs, 128), BF16),
            pltpu.VMEM((nx, deep, width), BF16),
            pltpu.VMEM((nx, deep, width), BF16),
            pltpu.VMEM((nx, RANK, width), BF16),
            pltpu.VMEM((nz, RANK, fe), BF16),
            pltpu.VMEM((nr, nz, RANK, fe), BF16),
            pltpu.VMEM((rows, fz), BF16),
            pltpu.VMEM((nz, SLOTS, 2 * RANK), F32),
            pltpu.VMEM((nz, SLOTS, 2 * RANK), F32),
            pltpu.VMEM((nx, SLOTS, 2 * RANK), F32),
            pltpu.VMEM((nz, 4 * lbo, 128), BF16),
            pltpu.VMEM((nz, 4 * lbo, 128), BF16),
            pltpu.VMEM((nz, 4 * lbo, 128), BF16),
            pltpu.VMEM((nz, 4 * lbo, 128), BF16),
            dma((6,)),
            dma((nz,)), dma((nz,)), dma((nx,)), dma((nx,)),
            dma((nx,)), dma((nx,)), dma((nx,)), dma((nx,)), dma((nx,)), dma((nx,)),
            dma((nx,)), dma((nx,)), dma((nx,)), dma((nx,)), dma((nx,)), dma((nx,)),
            dma((nr,)), dma((nr,)), dma((nz,)), dma((nz,)),
            dma((ny, ng)), dma((ny, ng)), dma((ny, ng)), dma((ny, ng)),
            dma((nz,)), dma((nz,)), dma((nx,)), dma((nx,)),
            dma((nz,)), dma((nz,)), dma((nz,)), dma((nz,)),
        ],
        compiler_params=pltpu.CompilerParams(
            collective_id=0, has_side_effects=True, vmem_limit_bytes=32 * 1024 * 1024
        ),
        cost_estimate=pl.CostEstimate(flops=2_000_000_000, bytes_accessed=4_000_000, transcendentals=0),
    )(xz, adapter_ids.reshape(1, rows // 2), key_weight, value_weight, dn, adapter_up[0])
    return key_out.reshape(steps, own, -1), value_out.reshape(steps, own, -1)


def solution(mesh):
    nr, tp = mesh.shape["rows"], mesh.shape["tp"]
    nx = 4 if tp >= 64 else 2
    placed = (
        P(None, ("rows", "tp"), None),
        P("rows", None),
        P("tp", None),
        P("tp", None),
        P("rows", "tp"),
        P("tp", None, None),
    )
    return jax.shard_map(
        functools.partial(shards, nr, tp // nx, nx),
        mesh=mesh,
        in_specs=placed,
        out_specs=(P(None, ("rows", "tp"), None), P(None, ("rows", "tp"), None)),
        check_vma=False,
    )
```

time: 528 us -> 74 us (0.14)
  the two profiles are of different devices: /device:TPU:8 before, /device:TPU:32 now
where the time goes in v2:
time: 74 us; the launch traced here: 73.9 us
  Pallas kernels  69.7 us (94%)
  local copies, waits for them, and re-layouts  3.4 us (5%)
    pallas_call x1, Pallas kernels, shards(): pl.pallas_call(functools.partial(kernel, nr, nz, nx, ng), out_shape=[jax....  69.7 us
    unnamed x11, local copies, waits for them, and re-layouts  1.98 us

profile of v2, /device:TPU:32, one launch (start us, length us, event | category | flops | bytes accessed | tf_op | source)
XLA Modules:
  0.0 73.9 jit_solution(17638326356282059840)
XLA Ops:
  0.6 0.0 copy-start.4
  0.6 0.0 copy-start.2
  0.6 1.0 %copy.11 = bf16[8,8,16,128]{3,2,1,0:T(8,128)(2,1)S(1)} copy(bf16[8,8,16,128]{3,1,2,0:T(8,128)(2,1)} %bitcast.20) | data formatting | bytes 524288
  1.7 0.0 copy-start
  1.7 0.0 copy-start.1
  1.7 0.1 copy.14
  1.8 0.0 copy-done.4
  1.8 0.1 reshape.22
  1.9 0.0 copy-start.3
  2.0 0.0 copy-done.2
  2.0 0.8 %copy-done = bf16[256,1024]{1,0:T(8,128)(2,1)S(1)} copy-done((bf16[256,1024]{1,0:T(8,128)(2,1)S(1)}, bf16[256,1024]{1,0:T(8,128)(2,1)}, u32[]{:S(2)}) %copy-start) | copy-done | bytes 524312
  2.7 0.2 copy-done.1
  2.9 0.0 copy-done.3
  2.9 69.7 %shard_map.77 = (bf16[32,128]{1,0:T(8,128)(2,1)S(1)}, bf16[32,128]{1,0:T(8,128)(2,1)S(1)}) custom-call(bf16[16,32,128]{2,1,0:T(8,128)(2,1)S(1)} %bitcast.16, s32[1,128]{1,0:T(1,128)S(1)} %bitcast.18, bf16[256,1024]{1,0:T(8,128)(2,1)S(1)} %copy-done, bf16[256,1024]{1,0:T(8,128)(2,1)S(1)} %copy-done.1, bf16[8,2,64,128]{3,2,1,0:T(8,128)(2,1)S(1)} %bitcast.15, ...), custom_call_target="tpu_custom_call" | custom-call | flops 2000000000 | bytes 4000000 | tf_op jit(solution)/shard_map/pallas_call | solution.py:418
  72.6 0.6 reshape.26
  73.3 0.6 reshape.27
  (1 shorter events, 0.0 us)
Async XLA Ops:
  0.6 1.2 %copy-start.4 = (bf16[2,2,16384]{2,1,0:T(2,128)(2,1)S(1)}, bf16[2,2,16384]{2,1,0:T(2,128)(2,1)}, u32[]{:S(2)}) copy-start(bf16[2,2,16384]{2,1,0:T(2,128)(2,1)} %param.6) | copy-start | bytes 393220
  0.6 1.3 %copy-start.2 = (bf16[1,64,1024]{2,1,0:T(8,128)(2,1)S(1)}, bf16[1,64,1024]{2,1,0:T(8,128)(2,1)}, u32[]{:S(2)}) copy-start(bf16[1,64,1024]{2,1,0:T(8,128)(2,1)} %param.11) | copy-start | bytes 393220
  1.7 1.0 %copy-start = (bf16[256,1024]{1,0:T(8,128)(2,1)S(1)}, bf16[256,1024]{1,0:T(8,128)(2,1)}, u32[]{:S(2)}) copy-start(bf16[256,1024]{1,0:T(8,128)(2,1)} %wk_ref.1) | copy-start | bytes 1572868
  1.7 1.2 %copy-start.1 = (bf16[256,1024]{1,0:T(8,128)(2,1)S(1)}, bf16[256,1024]{1,0:T(8,128)(2,1)}, u32[]{:S(2)}) copy-start(bf16[256,1024]{1,0:T(8,128)(2,1)} %wv_ref.1) | copy-start | bytes 1572868
  1.9 1.0 %copy-start.3 = (s32[128,1]{0,1:T(1,128)S(1)}, s32[128,1]{0,1:T(1,128)}, u32[]{:S(2)}) copy-start(s32[128,1]{0,1:T(1,128)} %param.7) | copy-start | bytes 1540

commit v3 on v2

--- a/solution.py
+++ b/solution.py
@@ -27,7 +27,7 @@
     return n.bit_length() - 1
 
 
-TURNS = {16: (8, 7, 1, 0, 9, 6, 2, 15, 10, 5, 3, 14, 11, 4, 12, 13), 4: (2, 0, 1, 3)}
+TURNS = {16: (0, 1, 15, 2, 8, 7, 9, 6, 10, 5, 11, 4, 12, 3, 13, 14), 4: (2, 0, 1, 3)}
 
 
 def kernel(
@@ -121,9 +121,10 @@
     def share(n):
         return pl.ds(pl.multiple_of(c * (n // CORES), n // CORES), n // CORES)
 
-    def wk_copy(k):
-        some = share(deep)
-        return send(wk_ref.at[some], wkg.at[x, some], wk_s.at[k], wk_r.at[k], x_dev(at_x(k)))
+    def wk_copy(k, h):
+        few = deep // (2 * CORES)
+        some = pl.ds(pl.multiple_of(c * (deep // CORES) + h * few, few), few)
+        return send(wk_ref.at[some], wkg.at[x, some], wk_s.at[k, h], wk_r.at[k, h], x_dev(at_x(k)))
 
     def wv_copy(k):
         some = share(deep)
@@ -147,7 +148,8 @@
         return pass_on(ug, RANK, upc_s, upc_r, k)
 
     for k in range(1, nx):
-        wk_copy(k).start()
+        wk_copy(k, 0).start()
+        up_copy(k).start()
 
     group = rows // 2
     ids = jnp.broadcast_to(id_ref[...].astype(F32).astype(BF16), (8, group))
@@ -288,16 +290,14 @@
 
     for g in range(2, ng):
         over_z(g)
-        over_y(g - 2)
+    over_y(0)
 
     for k in range(1, nx):
         xx_copy(k).wait_recv()
     for k in range(1, nx):
+        wk_copy(k, 1).start()
+    for k in range(1, nx):
         wv_copy(k).start()
-        up_copy(k).start()
-    for k in range(1, nx):
-        wk_copy(k).wait_recv()
-        wkc_copy(k).start()
     zb = nz // 2
     wide = jnp.concatenate(
         [xg[:, 2 * b:2 * b + 2].reshape(block, 128) for b in range(zb)], axis=1
@@ -311,31 +311,31 @@
             ]
     picked = dot(gather, xm[...]).astype(BF16)
 
-    for g in range(ng - 2):
-        over_core(g)
-    over_y(ng - 2)
-
-    for k in range(1, nx):
-        wkc_copy(k).wait_recv()
-    for one in w_own:
-        one.wait()
-    x_rows = dot(own, xm[...]).astype(BF16)
-    ks[...] = parcels(dot(x_rows, wkg[...].reshape(nx * deep, width)).astype(BF16))
-    kr[nz - 1] = ks[z]
-    over_y(ng - 1)
-    over_core(ng - 2)
-    turns(lambda q: k_copy(q).start())
+    for g in range(1, ng):
+        over_y(g)
+        over_core(g - 1)
     for g in range(ng - 2):
         shrink(g, picked)
     over_core(ng - 1)
     shrink(ng - 2, picked)
     shrink(ng - 1, picked)
-    for k in range(1, nx):
-        wv_copy(k).wait_recv()
+
+    for k in range(1, nx):
+        for h in range(2):
+            wk_copy(k, h).wait_recv()
+        wkc_copy(k).start()
+    x_rows = dot(own, xm[...]).astype(BF16)
+    for one in w_own:
+        one.wait()
+    for k in range(1, nx):
+        wkc_copy(k).wait_recv()
+    ks[...] = parcels(dot(x_rows, wkg[...].reshape(nx * deep, width)).astype(BF16))
+    turns(lambda q: k_copy(q).start())
+    kr[nz - 1] = ks[z]
+
+    for k in range(1, nx):
         up_copy(k).wait_recv()
-        wvc_copy(k).start()
         upc_copy(k).start()
-
     for q in range(nz):
         if hops[q]:
             s_copy(q).wait_recv()
@@ -346,6 +346,9 @@
 
     for k in range(1, nx):
         sh_copy(k).start()
+    for k in range(1, nx):
+        wv_copy(k).wait_recv()
+        wvc_copy(k).start()
     for k in range(1, nx):
         wvc_copy(k).wait_recv()
         upc_copy(k).wait_recv()
@@ -374,7 +377,9 @@
     for k in range(1, nr):
         dr_copy(k).wait_send()
     for k in range(1, nx):
-        for one in (wk_copy, wv_copy, up_copy, wkc_copy, wvc_copy, upc_copy):
+        for h in range(2):
+            wk_copy(k, h).wait_send()
+        for one in (wv_copy, up_copy, wkc_copy, wvc_copy, upc_copy):
             one(k).wait_send()
         xx_copy(k).wait_send()
         sh_copy(k).wait_send()
@@ -437,7 +442,7 @@
             pltpu.VMEM((nz, 4 * lbo, 128), BF16),
             dma((6,)),
             dma((nz,)), dma((nz,)), dma((nx,)), dma((nx,)),
-            dma((nx,)), dma((nx,)), dma((nx,)), dma((nx,)), dma((nx,)), dma((nx,)),
+            dma((nx, 2)), dma((nx, 2)), dma((nx,)), dma((nx,)), dma((nx,)), dma((nx,)),
             dma((nx,)), dma((nx,)), dma((nx,)), dma((nx,)), dma((nx,)), dma((nx,)),
             dma((nr,)), dma((nr,)), dma((nz,)), dma((nz,)),
             dma((ny, ng)), dma((ny, ng)), dma((ny, ng)), dma((ny, ng)),

time: 74 us -> 71.9 us (0.972)
  Pallas kernels: 69.7 us -> 67.7 us
    pallas_call x1, Pallas kernels: 69.7 us -> 67.7 us  [shards(): pl.pallas_call(functools.partial(kernel, nr, nz, nx, ng), out_shape=[jax....]
where the time goes in v3:
time: 71.9 us; the launch traced here: 71.8 us
  Pallas kernels  67.7 us (94%)
  local copies, waits for them, and re-layouts  3.4 us (5%)
  between operations  0.72 us (1%)
    pallas_call x1, Pallas kernels, shards(): pl.pallas_call(functools.partial(kernel, nr, nz, nx, ng), out_shape=[jax....  67.7 us
    unnamed x11, local copies, waits for them, and re-layouts  1.98 us

profile of v3, /device:TPU:32, one launch (start us, length us, event | category | flops | bytes accessed | tf_op | source)
XLA Modules:
  0.0 71.8 jit_solution(4285737196331621564)
XLA Ops:
  0.6 0.0 copy-start.4
  0.6 0.0 copy-start.2
  0.6 1.0 %copy.11 = bf16[8,8,16,128]{3,2,1,0:T(8,128)(2,1)S(1)} copy(bf16[8,8,16,128]{3,1,2,0:T(8,128)(2,1)} %bitcast.20) | data formatting | bytes 524288
  1.7 0.0 copy-start
  1.7 0.0 copy-start.1
  1.7 0.1 copy.14
  1.8 0.0 copy-done.4
  1.8 0.1 reshape.22
  1.9 0.0 copy-start.3
  2.0 0.0 copy-done.2
  2.0 0.8 %copy-done = bf16[256,1024]{1,0:T(8,128)(2,1)S(1)} copy-done((bf16[256,1024]{1,0:T(8,128)(2,1)S(1)}, bf16[256,1024]{1,0:T(8,128)(2,1)}, u32[]{:S(2)}) %copy-start) | copy-done | bytes 524312
  2.7 0.2 copy-done.1
  2.9 0.0 copy-done.3
  2.9 67.7 %shard_map.77 = (bf16[32,128]{1,0:T(8,128)(2,1)S(1)}, bf16[32,128]{1,0:T(8,128)(2,1)S(1)}) custom-call(bf16[16,32,128]{2,1,0:T(8,128)(2,1)S(1)} %bitcast.16, s32[1,128]{1,0:T(1,128)S(1)} %bitcast.18, bf16[256,1024]{1,0:T(8,128)(2,1)S(1)} %copy-done, bf16[256,1024]{1,0:T(8,128)(2,1)S(1)} %copy-done.1, bf16[8,2,64,128]{3,2,1,0:T(8,128)(2,1)S(1)} %bitcast.15, ...), custom_call_target="tpu_custom_call" | custom-call | flops 2000000000 | bytes 4000000 | tf_op jit(solution)/shard_map/pallas_call | solution.py:423
  70.6 0.6 reshape.26
  71.2 0.6 reshape.27
  (1 shorter events, 0.0 us)
Async XLA Ops:
  0.6 1.2 %copy-start.4 = (bf16[2,2,16384]{2,1,0:T(2,128)(2,1)S(1)}, bf16[2,2,16384]{2,1,0:T(2,128)(2,1)}, u32[]{:S(2)}) copy-start(bf16[2,2,16384]{2,1,0:T(2,128)(2,1)} %param.6) | copy-start | bytes 393220
  0.6 1.3 %copy-start.2 = (bf16[1,64,1024]{2,1,0:T(8,128)(2,1)S(1)}, bf16[1,64,1024]{2,1,0:T(8,128)(2,1)}, u32[]{:S(2)}) copy-start(bf16[1,64,1024]{2,1,0:T(8,128)(2,1)} %param.11) | copy-start | bytes 393220
  1.7 1.0 %copy-start = (bf16[256,1024]{1,0:T(8,128)(2,1)S(1)}, bf16[256,1024]{1,0:T(8,128)(2,1)}, u32[]{:S(2)}) copy-start(bf16[256,1024]{1,0:T(8,128)(2,1)} %wk_ref.1) | copy-start | bytes 1572868
  1.7 1.2 %copy-start.1 = (bf16[256,1024]{1,0:T(8,128)(2,1)S(1)}, bf16[256,1024]{1,0:T(8,128)(2,1)}, u32[]{:S(2)}) copy-start(bf16[256,1024]{1,0:T(8,128)(2,1)} %wv_ref.1) | copy-start | bytes 1572868
  1.9 1.0 %copy-start.3 = (s32[128,1]{0,1:T(1,128)S(1)}, s32[128,1]{0,1:T(1,128)}, u32[]{:S(2)}) copy-start(s32[128,1]{0,1:T(1,128)} %param.7) | copy-start | bytes 1540

commit v4 on v3

--- a/solution.py
+++ b/solution.py
@@ -272,9 +272,11 @@
         for j in range(ny):
             dc_copy(j, g).wait_recv()
         acc = jnp.zeros((2 * half, qg * RANK), F32)
-        for e in range(nr):
-            block_d = dg[e, g * qg:(g + 1) * qg].reshape(qg * RANK, fe)
-            acc = acc + dot_t(picked[2 * half * g:2 * half * (g + 1), e * fe:(e + 1) * fe], block_d)
+        for e in range(0, nr, 2):
+            block_d = jnp.concatenate(
+                [dg[e + b, g * qg:(g + 1) * qg].reshape(qg * RANK, fe) for b in range(2)], axis=1
+            )
+            acc = acc + dot_t(picked[2 * half * g:2 * half * (g + 1), e * fe:(e + 2) * fe], block_d)
         for a in range(qg):
             first = acc[a * SLOTS:(a + 1) * SLOTS, a * RANK:(a + 1) * RANK]
             second = acc[half + a * SLOTS:half + (a + 1) * SLOTS, a * RANK:(a + 1) * RANK]
@@ -313,7 +315,9 @@
 
     for g in range(1, ng):
         over_y(g)
-        over_core(g - 1)
+        if g > 1:
+            over_core(g - 2)
+    over_core(ng - 2)
     for g in range(ng - 2):
         shrink(g, picked)
     over_core(ng - 1)
@@ -357,13 +361,18 @@
     row_l = lax.broadcasted_iota(jnp.int32, (tail, 2 * RANK), 0)
     mine = ((row_l >> 1) & 1) == (lane >= RANK).astype(jnp.int32)
     spot_o = lax.broadcasted_iota(jnp.int32, (tail, nx * SLOTS), 1) >> 3
+    places = [jnp.where(spot_o == xa, place, 0.0).astype(BF16) for xa in range(nx)]
     for k in range(1, nx):
         sh_copy(k).wait_recv()
     shrinks = sh[...].reshape(nx * SLOTS, 2 * RANK).astype(BF16)
+    lows = []
     for xa in range(nx):
-        place_a = jnp.where(spot_o == xa, place, 0.0).astype(BF16)
-        low_a = jnp.where(mine, dot(place_a, shrinks), 0.0).astype(BF16)
-        vp = vp + dot(low_a, jnp.concatenate([ug[xa], ug[xa]], axis=0))
+        low_a = jnp.where(mine, dot(places[xa], shrinks), 0.0)
+        lows.append(low_a + jnp.concatenate([low_a[:, RANK:], low_a[:, :RANK]], axis=1))
+    low = jnp.concatenate(
+        [jnp.where(lane < RANK, lows[xa], lows[xa + 1]) for xa in range(0, nx, 2)], axis=1
+    ).astype(BF16)
+    vp = vp + dot(low, ug[...].reshape(nx * RANK, width))
     vs[...] = parcels(vp.astype(BF16))
 
     def v_copy(q):

time: 71.9 us -> 71.2 us (level)
  the two profiles are of different devices: /device:TPU:32 before, /device:TPU:1 now
where the time goes in v4:
time: 71.2 us; the launch traced here: 70.3 us
  Pallas kernels  66.2 us (93%)
  local copies, waits for them, and re-layouts  3.4 us (5%)
  between operations  0.72 us (1%)
    pallas_call x1, Pallas kernels, shards(): pl.pallas_call(functools.partial(kernel, nr, nz, nx, ng), out_shape=[jax....  66.2 us
    unnamed x11, local copies, waits for them, and re-layouts  1.98 us

profile of v4, /device:TPU:1, one launch (start us, length us, event | category | flops | bytes accessed | tf_op | source)
XLA Modules:
  0.0 70.3 jit_solution(11617796296578343829)
XLA Ops:
  0.6 0.0 copy-start.4
  0.6 0.0 copy-start.2
  0.6 1.0 %copy.11 = bf16[8,8,16,128]{3,2,1,0:T(8,128)(2,1)S(1)} copy(bf16[8,8,16,128]{3,1,2,0:T(8,128)(2,1)} %bitcast.20) | data formatting | bytes 524288
  1.7 0.0 copy-start
  1.7 0.0 copy-start.1
  1.7 0.1 copy.14
  1.8 0.0 copy-done.4
  1.8 0.1 reshape.22
  1.9 0.0 copy-start.3
  2.0 0.0 copy-done.2
  2.0 0.8 %copy-done = bf16[256,1024]{1,0:T(8,128)(2,1)S(1)} copy-done((bf16[256,1024]{1,0:T(8,128)(2,1)S(1)}, bf16[256,1024]{1,0:T(8,128)(2,1)}, u32[]{:S(2)}) %copy-start) | copy-done | bytes 524312
  2.7 0.2 copy-done.1
  2.9 0.0 copy-done.3
  2.9 66.2 %shard_map.77 = (bf16[32,128]{1,0:T(8,128)(2,1)S(1)}, bf16[32,128]{1,0:T(8,128)(2,1)S(1)}) custom-call(bf16[16,32,128]{2,1,0:T(8,128)(2,1)S(1)} %bitcast.16, s32[1,128]{1,0:T(1,128)S(1)} %bitcast.18, bf16[256,1024]{1,0:T(8,128)(2,1)S(1)} %copy-done, bf16[256,1024]{1,0:T(8,128)(2,1)S(1)} %copy-done.1, bf16[8,2,64,128]{3,2,1,0:T(8,128)(2,1)S(1)} %bitcast.15, ...), custom_call_target="tpu_custom_call" | custom-call | flops 2000000000 | bytes 4000000 | tf_op jit(solution)/shard_map/pallas_call | solution.py:432
  69.1 0.6 reshape.26
  69.7 0.6 reshape.27
  (1 shorter events, 0.0 us)
Async XLA Ops:
  0.6 1.2 %copy-start.4 = (bf16[2,2,16384]{2,1,0:T(2,128)(2,1)S(1)}, bf16[2,2,16384]{2,1,0:T(2,128)(2,1)}, u32[]{:S(2)}) copy-start(bf16[2,2,16384]{2,1,0:T(2,128)(2,1)} %param.6) | copy-start | bytes 393220
  0.6 1.3 %copy-start.2 = (bf16[1,64,1024]{2,1,0:T(8,128)(2,1)S(1)}, bf16[1,64,1024]{2,1,0:T(8,128)(2,1)}, u32[]{:S(2)}) copy-start(bf16[1,64,1024]{2,1,0:T(8,128)(2,1)} %param.11) | copy-start | bytes 393220
  1.7 1.0 %copy-start = (bf16[256,1024]{1,0:T(8,128)(2,1)S(1)}, bf16[256,1024]{1,0:T(8,128)(2,1)}, u32[]{:S(2)}) copy-start(bf16[256,1024]{1,0:T(8,128)(2,1)} %wk_ref.1) | copy-start | bytes 1572868
  1.7 1.2 %copy-start.1 = (bf16[256,1024]{1,0:T(8,128)(2,1)S(1)}, bf16[256,1024]{1,0:T(8,128)(2,1)}, u32[]{:S(2)}) copy-start(bf16[256,1024]{1,0:T(8,128)(2,1)} %wv_ref.1) | copy-start | bytes 1572868
  1.9 1.0 %copy-start.3 = (s32[128,1]{0,1:T(1,128)S(1)}, s32[128,1]{0,1:T(1,128)}, u32[]{:S(2)}) copy-start(s32[128,1]{0,1:T(1,128)} %param.7) | copy-start | bytes 1540

commit v5 on v4

--- a/solution.py
+++ b/solution.py
@@ -27,7 +27,7 @@
     return n.bit_length() - 1
 
 
-TURNS = {16: (0, 1, 15, 2, 8, 7, 9, 6, 10, 5, 11, 4, 12, 3, 13, 14), 4: (2, 0, 1, 3)}
+TURNS = {16: (8, 0, 1, 15, 7, 9, 2, 14, 6, 10, 3, 13, 5, 11, 4, 12), 4: (2, 0, 1, 3)}
 
 
 def kernel(

time: 71.2 us -> 70.3 us (0.987)
  Pallas kernels: 66.2 us -> 65.1 us
    pallas_call x1, Pallas kernels: 66.2 us -> 65.1 us  [shards(): pl.pallas_call(functools.partial(kernel, nr, nz, nx, ng), out_shape=[jax....]
where the time goes in v5:
time: 70.3 us; the launch traced here: 69.3 us
  Pallas kernels  65.1 us (93%)
  local copies, waits for them, and re-layouts  3.4 us (5%)
  between operations  0.72 us (1%)
    pallas_call x1, Pallas kernels, shards(): pl.pallas_call(functools.partial(kernel, nr, nz, nx, ng), out_shape=[jax....  65.1 us
    unnamed x11, local copies, waits for them, and re-layouts  1.98 us

profile of v5, /device:TPU:1, one launch (start us, length us, event | category | flops | bytes accessed | tf_op | source)
XLA Modules:
  0.0 69.3 jit_solution(8301233309478589093)
XLA Ops:
  0.6 0.0 copy-start.4
  0.6 0.0 copy-start.2
  0.6 1.0 %copy.11 = bf16[8,8,16,128]{3,2,1,0:T(8,128)(2,1)S(1)} copy(bf16[8,8,16,128]{3,1,2,0:T(8,128)(2,1)} %bitcast.20) | data formatting | bytes 524288
  1.7 0.0 copy-start
  1.7 0.0 copy-start.1
  1.7 0.1 copy.14
  1.8 0.0 copy-done.4
  1.8 0.1 reshape.22
  1.9 0.0 copy-start.3
  2.0 0.0 copy-done.2
  2.0 0.8 %copy-done = bf16[256,1024]{1,0:T(8,128)(2,1)S(1)} copy-done((bf16[256,1024]{1,0:T(8,128)(2,1)S(1)}, bf16[256,1024]{1,0:T(8,128)(2,1)}, u32[]{:S(2)}) %copy-start) | copy-done | bytes 524312
  2.7 0.2 copy-done.1
  2.9 0.0 copy-done.3
  2.9 65.1 %shard_map.77 = (bf16[32,128]{1,0:T(8,128)(2,1)S(1)}, bf16[32,128]{1,0:T(8,128)(2,1)S(1)}) custom-call(bf16[16,32,128]{2,1,0:T(8,128)(2,1)S(1)} %bitcast.16, s32[1,128]{1,0:T(1,128)S(1)} %bitcast.18, bf16[256,1024]{1,0:T(8,128)(2,1)S(1)} %copy-done, bf16[256,1024]{1,0:T(8,128)(2,1)S(1)} %copy-done.1, bf16[8,2,64,128]{3,2,1,0:T(8,128)(2,1)S(1)} %bitcast.15, ...), custom_call_target="tpu_custom_call" | custom-call | flops 2000000000 | bytes 4000000 | tf_op jit(solution)/shard_map/pallas_call | solution.py:432
  68.0 0.6 reshape.26
  68.6 0.6 reshape.27
  (1 shorter events, 0.0 us)
Async XLA Ops:
  0.6 1.2 %copy-start.4 = (bf16[2,2,16384]{2,1,0:T(2,128)(2,1)S(1)}, bf16[2,2,16384]{2,1,0:T(2,128)(2,1)}, u32[]{:S(2)}) copy-start(bf16[2,2,16384]{2,1,0:T(2,128)(2,1)} %param.6) | copy-start | bytes 393220
  0.6 1.3 %copy-start.2 = (bf16[1,64,1024]{2,1,0:T(8,128)(2,1)S(1)}, bf16[1,64,1024]{2,1,0:T(8,128)(2,1)}, u32[]{:S(2)}) copy-start(bf16[1,64,1024]{2,1,0:T(8,128)(2,1)} %param.11) | copy-start | bytes 393220
  1.7 1.0 %copy-start = (bf16[256,1024]{1,0:T(8,128)(2,1)S(1)}, bf16[256,1024]{1,0:T(8,128)(2,1)}, u32[]{:S(2)}) copy-start(bf16[256,1024]{1,0:T(8,128)(2,1)} %wk_ref.1) | copy-start | bytes 1572868
  1.7 1.2 %copy-start.1 = (bf16[256,1024]{1,0:T(8,128)(2,1)S(1)}, bf16[256,1024]{1,0:T(8,128)(2,1)}, u32[]{:S(2)}) copy-start(bf16[256,1024]{1,0:T(8,128)(2,1)} %wv_ref.1) | copy-start | bytes 1572868
  1.9 1.0 %copy-start.3 = (s32[128,1]{0,1:T(1,128)S(1)}, s32[128,1]{0,1:T(1,128)}, u32[]{:S(2)}) copy-start(s32[128,1]{0,1:T(1,128)} %param.7) | copy-start | bytes 1540
